TPU v7x, 32 devices: a whole 2x2x4 slice. The times are simulated.
32 devices in a mesh: pair: 16 (over z, y, x), vir: 2 (over core).
Axes of the slice: x: 2, y: 2, z: 4, core: 2. Of those that a mesh axis runs over, the one named last changes fastest.
Arguments:
- amplitudes: bfloat16 [40960, 1024], P('pair', 'vir'), may hold values from -6 to 6
- cycle_ints: bfloat16 [40960, 1024], P('pair', 'vir'), may hold values from -6 to 6
- int_rows: bfloat16 [1024, 1024], P('pair', 'vir'), may hold values from -6 to 6
- row_dest: int32 [1024, 2], P('pair'), may hold values from 0 to 15, all different within a row; in each aligned block of 64 rows (0 to 63, 64 to 127, ...) at most 16 rows name the same one
- vir_energy: float32 [1024], P('vir'), may hold values from 0.5 to 4
- occ_energy: float32 [40960], P('pair'), may hold values from -2 to -0.2
Outputs:
- residual: bfloat16 [40960, 1024], P('pair', 'vir')
Inputs may be any that keep to these rules, and one draw needn't show every extreme that they name: `row_dest`: each integral row names 2 different pair groups; among the 64 rows of one pair group no group is named more than 16 times, a bound that some block reaches.
All inputs are finite; a program needn't handle non-finite values.
Results may differ from a plain program's by a relative error of at most 0.008.
Values may be sent and summed in bfloat16 or wider, within the bound.
A program may use at most 64 MiB of HBM per device.

v0:
```python
import math

import jax
import jax.numpy as jnp
from jax import lax
from jax.experimental import pallas as pl
from jax.experimental.pallas import tpu as pltpu
from jax.sharding import PartitionSpec as P

SLOTS = 256


def dispatch(int_rows, row_dest, groups, capacity):
    rows = int_rows.shape[0]
    group = jnp.arange(groups, dtype=jnp.int32)
    member = jnp.any(row_dest[None, :, :] == group[:, None, None], axis=2)
    before = jnp.arange(rows)[:, None] < jnp.arange(rows)[None, :]
    rank = jnp.dot(
        member.astype(jnp.bfloat16), before.astype(jnp.bfloat16), preferred_element_type=jnp.float32
    ).astype(jnp.int32)
    slot = jnp.arange(capacity, dtype=jnp.int32)
    select = member[:, None, :] & (rank[:, None, :] == slot[None, :, None])
    select = select.reshape(groups * capacity, rows).astype(int_rows.dtype)
    return jnp.dot(select, int_rows, preferred_element_type=jnp.float32).astype(int_rows.dtype)


def body(amplitudes, cycle_ints, int_rows, row_dest, vir_energy, occ_energy):
    groups = lax.axis_size("pair")
    row_count, local_width = amplitudes.shape
    full_width = local_width * lax.axis_size("vir")
    capacity = SLOTS // groups
    gathered = lax.all_gather(amplitudes, "vir", axis=1, tiled=True)
    cross_part = lax.dot_general(
        gathered, cycle_ints, (((0,), (0,)), ((), ())), preferred_element_type=jnp.float32
    )
    scale_cycle = math.sqrt(row_count * groups * full_width)
    cross_half = lax.psum((cross_part / scale_cycle).astype(jnp.bfloat16), "pair")
    outgoing = dispatch(int_rows, row_dest, groups, capacity)
    arrived = lax.all_to_all(
        outgoing.reshape(groups, capacity, local_width),
        "pair",
        split_axis=0,
        concat_axis=0,
        tiled=True,
    ).reshape(groups * capacity, local_width)
    chosen = lax.all_gather(arrived, "vir", axis=1, tiled=True)
    coefficient = lax.dot_general(
        gathered, chosen, (((1,), (1,)), ((), ())), preferred_element_type=jnp.float32
    ) / math.sqrt(full_width)
    ladder = jnp.dot(
        coefficient.astype(jnp.bfloat16), arrived, preferred_element_type=jnp.float32
    ) / math.sqrt(SLOTS)
    energy = (vir_energy[None, :] - occ_energy[:, None]) * amplitudes.astype(jnp.float32)
    cycle_term = jnp.dot(gathered, cross_half, preferred_element_type=jnp.float32)
    return (cycle_term + ladder + energy).astype(jnp.bfloat16)


DEPTH, PLANE, HALVES, PIECES = 4, 4, 2, 4
F32, BF16 = jnp.float32, jnp.bfloat16


def rows_at(start, size):
    return pl.ds(pl.multiple_of(start, size), size)


def kernel(
    amp_hbm, cyc_hbm, rows_hbm, dest_hbm, vir_hbm, occ_hbm, out,
    amp, cyc, rows, dest, vir_e, occ_e, other, part, plane_in, zsum, z_in, full, outgoing, arr, arr_o, acc,
    load_sem, amp_sem, route_sem, arr_sem, plane_sem, z_sem, gz_sem, gp_sem,
):
    groups = DEPTH * PLANE
    me, v = lax.axis_index("pair"), lax.axis_index("vir")
    z, q = me // PLANE, me % PLANE
    count, width = amp.shape
    full_width = 2 * width
    capacity = SLOTS // groups
    half = width // HALVES
    block = full_width // PLANE
    piece = block // DEPTH

    loads = [
        pltpu.make_async_copy(src, dst, load_sem.at[i])
        for i, (src, dst) in enumerate(
            (
                (dest_hbm, dest), (rows_hbm, rows), (vir_hbm, vir_e), (occ_hbm, occ_e),
                (amp_hbm, amp), (cyc_hbm, cyc),
            )
        )
    ]
    for c in loads:
        c.start()
    barrier = pltpu.get_barrier_semaphore()
    for k in range(1, groups):
        pl.semaphore_signal(
            barrier, inc=1, device_id=((me + k) % groups, v), device_id_type=pl.DeviceIdType.MESH
        )
    pl.semaphore_signal(barrier, inc=1, device_id=(me, 1 - v), device_id_type=pl.DeviceIdType.MESH)

    def copy(src, dst, sem, index, device):
        return pltpu.make_async_remote_copy(
            src_ref=src,
            dst_ref=dst,
            send_sem=sem.at[(0, *index)],
            recv_sem=sem.at[(1, *index)],
            device_id=device,
            device_id_type=pl.DeviceIdType.MESH,
        )

    loads[0].wait()
    loads[1].wait()
    group = lax.broadcasted_iota(jnp.int32, (SLOTS, rows.shape[0]), 0) // capacity
    slot = lax.broadcasted_iota(jnp.int32, (SLOTS, rows.shape[0]), 0) % capacity
    member = group == dest[0:1, :]
    for k in range(1, dest.shape[0]):
        member = member | (group == dest[k : k + 1, :])
    tri = (rows.shape[0], rows.shape[0])
    before = lax.broadcasted_iota(jnp.int32, tri, 0) < lax.broadcasted_iota(jnp.int32, tri, 1)
    rank = jnp.dot(
        jnp.where(member, 1.0, 0.0).astype(BF16),
        jnp.where(before, 1.0, 0.0).astype(BF16),
        preferred_element_type=F32,
    )
    select = jnp.where(member & (rank == slot.astype(F32)), 1.0, 0.0).astype(BF16)
    outgoing[...] = jnp.dot(select, rows[...], preferred_element_type=F32).astype(BF16)
    pl.semaphore_wait(barrier, groups)

    step = count // PIECES
    amp_copies = [
        copy(amp_hbm.at[pl.ds(i * step, step)], other.at[pl.ds(i * step, step)], amp_sem, (i,), (me, 1 - v))
        for i in range(PIECES)
    ]
    for c in amp_copies:
        c.start()
    route_copies = []
    for k in range(1, groups):
        to = (me + k) % groups
        c = copy(
            outgoing.at[rows_at(to * capacity, capacity)],
            arr.at[rows_at(me * capacity, capacity)],
            route_sem, (k - 1,), (to, v),
        )
        c.start()
        route_copies.append(c)
    mine = rows_at(me * capacity, capacity)
    arr[mine, :] = outgoing[mine, :]

    plane_copies = [
        [
            [
                copy(
                    part.at[h, rows_at(((q + d) % PLANE * DEPTH + (z + e) % DEPTH) * piece, piece)],
                    plane_in.at[h, d - 1, rows_at((z + e) % DEPTH * piece, piece)],
                    plane_sem, (h, e % DEPTH, d - 1), (z * PLANE + (q + d) % PLANE, v),
                )
                for e in range(1, DEPTH + 1)
            ]
            for d in range(1, PLANE)
        ]
        for h in range(HALVES)
    ]

    def cross(src, owner, h):
        for j in range(width // block):
            value = lax.dot_general(
                src[:, pl.ds(j * block, block)],
                cyc[:, pl.ds(h * half, half)],
                (((0,), (0,)), ((), ())),
                preferred_element_type=F32,
            )
            part[h, rows_at(owner * width + j * block, block), :] = value.astype(BF16)
        for d in range(1, PLANE):
            target = (q + d) % PLANE

            @pl.when(target // (PLANE // 2) == owner)
            def _():
                for c in plane_copies[h][d - 1]:
                    c.start()

    for c in loads[2:]:
        c.wait()
    for h in range(HALVES):
        cross(amp, v, h)
    for c in amp_copies:
        c.wait_recv()
    arr_copy = copy(arr, arr_o, arr_sem, (0,), (me, 1 - v))
    for h in range(HALVES):
        cross(other, 1 - v, h)
        if h == 0:
            for c in route_copies:
                c.wait_recv()
            arr_copy.start()
    tile = 256
    contract = (((1,), (1,)), ((), ()))

    def ladder(t, carry):
        at = rows_at(t * tile, tile)
        mine = amp[at, :]
        value = lax.dot_general(mine, arr[...], contract, preferred_element_type=F32)
        value += lax.dot_general(other[at, :], arr_o[...], contract, preferred_element_type=F32)
        value = (value / math.sqrt(full_width)).astype(BF16)
        value = jnp.dot(value, arr[...], preferred_element_type=F32) / math.sqrt(SLOTS)
        for s in range(tile // 128):
            line = jnp.broadcast_to(occ_e[pl.ds(t * (tile // 128) + s, 1), :], (128, 128)).T
            for b in range(width // 128):
                cols = slice(b * 128, (b + 1) * 128)
                sub = slice(s * 128, (s + 1) * 128)
                acc[pl.ds(pl.multiple_of(t * tile + s * 128, 128), 128), cols] = value[sub, cols] + (
                    vir_e[:, cols] - line
                ) * mine[sub, cols].astype(F32)
        return carry

    tiles = count // tile
    z_copies, gz_copies, gp_copies = [], [], []
    gp_h = [[] for _ in range(HALVES)]
    shares = 3 * HALVES - 1

    def some_ladder(i):
        lax.fori_loop(i * tiles // shares, (i + 1) * tiles // shares, ladder, 0)

    for h in range(HALVES):
        for e in range(1, DEPTH + 1):
            to = (z + e) % DEPTH
            for d in range(1, PLANE):
                plane_copies[h][d - 1][e - 1].wait_recv()
            at = rows_at(to * piece, piece)
            total = part[h, rows_at((q * DEPTH + to) * piece, piece), :].astype(F32)
            for d in range(1, PLANE):
                total += plane_in[h, d - 1, at, :].astype(F32)
            zsum[h, at, :] = total.astype(BF16)
            if e < DEPTH:
                c = copy(
                    zsum.at[h, at], z_in.at[h, e - 1], z_sem, (h, e - 1), (to * PLANE + q, v)
                )
                c.start()
                z_copies.append(c)
        if h == 0:
            arr_copy.wait_recv()
        some_ladder(h)
    def spread(h, e):
        at = rows_at((q * DEPTH + (z - e + DEPTH) % DEPTH) * piece, piece)
        for d in range(1, PLANE):
            c = copy(
                full.at[h, at], full.at[h, at],
                gp_sem, (h, e, d - 1), (z * PLANE + (q + d) % PLANE, v),
            )
            c.start()
            gp_copies.append(c)
            gp_h[h].append(c)

    scale = math.sqrt(count * groups * full_width)
    own = rows_at((q * DEPTH + z) * piece, piece)
    for h in range(HALVES):
        for e in range(1, DEPTH):
            z_copies[h * (DEPTH - 1) + e - 1].wait_recv()
        total = zsum[h, rows_at(z * piece, piece), :].astype(F32)
        for e in range(1, DEPTH):
            total += z_in[h, e - 1].astype(F32)
        full[h, own, :] = (total / scale).astype(BF16)
        for e in range(1, DEPTH):
            c = copy(
                full.at[h, own], full.at[h, own], gz_sem, (h, e - 1), ((z + e) % DEPTH * PLANE + q, v)
            )
            c.start()
            gz_copies.append(c)
        spread(h, 0)
        some_ladder(HALVES + h)
    for h in range(HALVES):
        for e in range(1, DEPTH):
            gz_copies[h * (DEPTH - 1) + e - 1].wait_recv()
            spread(h, e)
        if h < HALVES - 1:
            some_ladder(2 * HALVES + h)
    for h in range(HALVES):
        for c in gp_h[h]:
            c.wait_recv()
        cols = slice(h * half, (h + 1) * half)

        def cycle(t, carry):
            at = rows_at(t * tile, tile)
            value = jnp.dot(
                amp[at, :], full[h, rows_at(v * width, width), :], preferred_element_type=F32
            )
            value += jnp.dot(
                other[at, :], full[h, rows_at((1 - v) * width, width), :], preferred_element_type=F32
            )
            out[at, cols] = (value + acc[at, cols]).astype(BF16)
            return carry

        lax.fori_loop(0, tiles, cycle, 0)
    plane_all = [c for of_half in plane_copies for of_peer in of_half for c in of_peer]
    for c in amp_copies + route_copies + [arr_copy] + plane_all + z_copies + gz_copies + gp_copies:
        c.wait_send()


def fused(amplitudes, cycle_ints, int_rows, row_dest, vir_energy, occ_energy):
    count, width = amplitudes.shape
    groups = DEPTH * PLANE
    half, block = width // HALVES, 2 * width // PLANE
    dma = pltpu.SemaphoreType.DMA
    return pl.pallas_call(
        kernel,
        out_shape=jax.ShapeDtypeStruct((count, width), BF16),
        in_specs=[pl.BlockSpec(memory_space=pl.ANY)] * 6,
        out_specs=pl.BlockSpec(memory_space=pltpu.VMEM),
        scratch_shapes=[
            pltpu.VMEM((count, width), BF16),
            pltpu.VMEM((count, width), BF16),
            pltpu.VMEM(int_rows.shape, BF16),
            pltpu.VMEM(row_dest.shape[::-1], jnp.int32),
            pltpu.VMEM((1, width), F32),
            pltpu.VMEM((count // 128, 128), F32),
            pltpu.VMEM((count, width), BF16),
            pltpu.VMEM((HALVES, 2 * width, half), BF16),
            pltpu.VMEM((HALVES, PLANE - 1, block, half), BF16),
            pltpu.VMEM((HALVES, block, half), BF16),
            pltpu.VMEM((HALVES, DEPTH - 1, block // DEPTH, half), BF16),
            pltpu.VMEM((HALVES, 2 * width, half), BF16),
            pltpu.VMEM((SLOTS, width), BF16),
            pltpu.VMEM((SLOTS, width), BF16),
            pltpu.VMEM((SLOTS, width), BF16),
            pltpu.VMEM((count, width), F32),
            dma((6,)),
            dma((2, PIECES)),
            dma((2, groups - 1)),
            dma((2, 1)),
            dma((2, HALVES, DEPTH, PLANE - 1)),
            dma((2, HALVES, DEPTH - 1)),
            dma((2, HALVES, DEPTH - 1)),
            dma((2, HALVES, DEPTH, PLANE - 1)),
        ],
        compiler_params=pltpu.CompilerParams(
            collective_id=0, has_side_effects=True, vmem_limit_bytes=60 * 2**20
        ),
    )(
        amplitudes, cycle_ints, int_rows, row_dest.T,
        vir_energy.reshape(1, width), occ_energy.reshape(count // 128, 128),
    )


def solution(mesh):
    fits = mesh.shape["pair"] == DEPTH * PLANE and mesh.shape["vir"] == 2
    return jax.shard_map(
        fused if fits else body,
        mesh=mesh,
        in_specs=(
            P("pair", "vir"),
            P("pair", "vir"),
            P("pair", "vir"),
            P("pair", None),
            P("vir"),
            P("pair"),
        ),
        out_specs=P("pair", "vir"),
        check_vma=False,
    )
```

profile of v0, /device:TPU:0, one launch (start us, length us, event | category | flops | bytes accessed | tf_op | source)
XLA Modules:
  0.0 46.8 jit_solution(399994635584908994)
XLA Ops:
  0.0 43.4 %shard_map.64 = bf16[2560,512]{1,0:T(8,128)(2,1)} custom-call(bf16[2560,512]{1,0:T(8,128)(2,1)} %amp_hbm.1, bf16[2560,512]{1,0:T(8,128)(2,1)} %cyc_hbm.1, bf16[64,512]{1,0:T(8,128)(2,1)} %rows_hbm.1, s32[2,64]{1,0:T(2,128)} %bitcast.5, f32[1,512]{1,0:T(1,128)} %bitcast.4, f32[20,128]{1,0:T(8,128)} %bitcast.3), custom_call_target="tpu_custom_call" | custom-call | tf_op jit(solution)/shard_map/pallas_call | solution.py:300
  43.4 3.4 %copy.8 = bf16[2560,512]{1,0:T(8,128)(2,1)} copy(bf16[2560,512]{1,0:T(8,128)(2,1)} %shard_map.64) | data formatting | bytes 5242880
where the time goes:
time: 46.9 us; the launch traced here: 46.8 us
  Pallas kernels  43.4 us (93%)
  local copies, waits for them, and re-layouts  3.4 us (7%)
    pallas_call x1, Pallas kernels, fused(): pl.pallas_call(kernel, out_shape=jax.ShapeDtypeStruct((count, width), BF1...  43.4 us
    unnamed x1, local copies, waits for them, and re-layouts  3.4 us

commit v1 on v0

v1 whole, which is shorter than its diff:
```python
import math

import jax
import jax.numpy as jnp
from jax import lax
from jax.experimental import pallas as pl
from jax.experimental.pallas import tpu as pltpu
from jax.sharding import PartitionSpec as P

SLOTS = 256


def dispatch(int_rows, row_dest, groups, capacity):
    rows = int_rows.shape[0]
    group = jnp.arange(groups, dtype=jnp.int32)
    member = jnp.any(row_dest[None, :, :] == group[:, None, None], axis=2)
    before = jnp.arange(rows)[:, None] < jnp.arange(rows)[None, :]
    rank = jnp.dot(
        member.astype(jnp.bfloat16), before.astype(jnp.bfloat16), preferred_element_type=jnp.float32
    ).astype(jnp.int32)
    slot = jnp.arange(capacity, dtype=jnp.int32)
    select = member[:, None, :] & (rank[:, None, :] == slot[None, :, None])
    select = select.reshape(groups * capacity, rows).astype(int_rows.dtype)
    return jnp.dot(select, int_rows, preferred_element_type=jnp.float32).astype(int_rows.dtype)


def body(amplitudes, cycle_ints, int_rows, row_dest, vir_energy, occ_energy):
    groups = lax.axis_size("pair")
    row_count, local_width = amplitudes.shape
    full_width = local_width * lax.axis_size("vir")
    capacity = SLOTS // groups
    gathered = lax.all_gather(amplitudes, "vir", axis=1, tiled=True)
    cross_part = lax.dot_general(
        gathered, cycle_ints, (((0,), (0,)), ((), ())), preferred_element_type=jnp.float32
    )
    scale_cycle = math.sqrt(row_count * groups * full_width)
    cross_half = lax.psum((cross_part / scale_cycle).astype(jnp.bfloat16), "pair")
    outgoing = dispatch(int_rows, row_dest, groups, capacity)
    arrived = lax.all_to_all(
        outgoing.reshape(groups, capacity, local_width),
        "pair",
        split_axis=0,
        concat_axis=0,
        tiled=True,
    ).reshape(groups * capacity, local_width)
    chosen = lax.all_gather(arrived, "vir", axis=1, tiled=True)
    coefficient = lax.dot_general(
        gathered, chosen, (((1,), (1,)), ((), ())), preferred_element_type=jnp.float32
    ) / math.sqrt(full_width)
    ladder = jnp.dot(
        coefficient.astype(jnp.bfloat16), arrived, preferred_element_type=jnp.float32
    ) / math.sqrt(SLOTS)
    energy = (vir_energy[None, :] - occ_energy[:, None]) * amplitudes.astype(jnp.float32)
    cycle_term = jnp.dot(gathered, cross_half, preferred_element_type=jnp.float32)
    return (cycle_term + ladder + energy).astype(jnp.bfloat16)


DEPTH, PLANE, UNITS = 4, 4, 4
DIRECT_SUM = ()
DIRECT_SPREAD = (3,)
F32, BF16 = jnp.float32, jnp.bfloat16
MESH = pl.DeviceIdType.MESH


def rows_at(start, size):
    return pl.ds(pl.multiple_of(start, size), size)


def kernel(
    amp_hbm, cyc_hbm, rows_hbm, dest_hbm, vir_hbm, occ_hbm, other, acc, last,
    amp, cyc, rows, dest, vir_e, occ_e, part, first_in, passed, second_in, zsum, z_in, full,
    outgoing, arr, arr_o, gram,
    near_sem, far_sem, load_sem, amp_sem, route_sem, arr_sem, sum_sem, z_sem, gz_sem, spread_sem,
):
    groups = DEPTH * PLANE
    me, v = lax.axis_index("pair"), lax.axis_index("vir")
    z, y, x = me // PLANE, me % PLANE // 2, me % 2
    by_x, by_y, by_xy = me + 1 - 2 * x, me + 2 - 4 * y, z * PLANE + 3 - me % PLANE
    count, width = amp.shape
    full_width = 2 * width
    capacity = SLOTS // groups
    unit = full_width // UNITS
    block = unit // PLANE
    piece = block // DEPTH

    loads = [
        pltpu.make_async_copy(src, dst, load_sem.at[i])
        for i, (src, dst) in enumerate(
            (
                (dest_hbm, dest), (rows_hbm, rows), (amp_hbm, amp), (cyc_hbm, cyc),
                (vir_hbm, vir_e), (occ_hbm, occ_e),
            )
        )
    ]
    barrier = pltpu.get_barrier_semaphore()
    pl.semaphore_signal(barrier, inc=1, device_id=(me, 1 - v), device_id_type=MESH)
    for k in range(1, groups):
        to = (me + k) % groups
        hops = jnp.abs(to // PLANE - z) + jnp.abs(to % PLANE // 2 - y) + jnp.abs(to % 2 - x)
        core = jnp.where(hops == 1, 0, 1)
        pl.semaphore_signal(barrier, inc=1, device_id=(to, core), device_id_type=MESH)
    near = 2 + jnp.where(z > 0, 1, 0) + jnp.where(z < DEPTH - 1, 1, 0)
    for c in loads:
        c.start()

    started = []

    def copy(src, dst, sem, index, device):
        c = pltpu.make_async_remote_copy(
            src_ref=src,
            dst_ref=dst,
            send_sem=sem.at[(0, *index)],
            recv_sem=sem.at[(1, *index)],
            device_id=device,
            device_id_type=MESH,
        )
        c.start()
        started.append(c)
        return c

    loads[0].wait()
    loads[1].wait()
    group = lax.broadcasted_iota(jnp.int32, (SLOTS, rows.shape[0]), 0) // capacity
    slot = lax.broadcasted_iota(jnp.int32, (SLOTS, rows.shape[0]), 0) % capacity
    member = group == dest[0:1, :]
    for k in range(1, dest.shape[0]):
        member = member | (group == dest[k : k + 1, :])
    tri = (rows.shape[0], rows.shape[0])
    before = lax.broadcasted_iota(jnp.int32, tri, 0) < lax.broadcasted_iota(jnp.int32, tri, 1)
    rank = jnp.dot(
        jnp.where(member, 1.0, 0.0).astype(BF16),
        jnp.where(before, 1.0, 0.0).astype(BF16),
        preferred_element_type=F32,
    )
    select = jnp.where(member & (rank == slot.astype(F32)), 1.0, 0.0).astype(BF16)
    outgoing[...] = jnp.dot(select, rows[...], preferred_element_type=F32).astype(BF16)
    mine = rows_at(me * capacity, capacity)
    arr[mine, :] = outgoing[mine, :]

    def cross(u):
        src = amp if u < UNITS // 2 else other
        at = u % (UNITS // 2) * unit
        part[u] = lax.dot_general(
            src[:, at : at + unit], cyc[...], (((0,), (0,)), ((), ())), preferred_element_type=F32
        ).astype(BF16)

    def axes(u):
        return (x, y, by_x, by_y) if u % 2 == 0 else (y, x, by_y, by_x)

    def quarter(a, b):
        return rows_at((a * 2 + b) * block, block)

    sums = {}

    def sum_first(u):
        a, b, by_a, by_b = axes(u)
        if u in DIRECT_SUM:
            sums[u, 0] = copy(
                part.at[u, quarter(1 - a, 1 - b)], first_in.at[u, 0], sum_sem, (u, 0), (by_xy, v)
            )
            sums[u, 2] = copy(
                part.at[u, quarter(a, 1 - b)], second_in.at[u], sum_sem, (u, 2), (by_b, v)
            )
        else:
            sums[u, 0] = copy(
                part.at[u, quarter(1 - a, 1 - b)], first_in.at[u, 0], sum_sem, (u, 0), (by_a, v)
            )
        sums[u, 1] = copy(
            part.at[u, quarter(1 - a, b)], first_in.at[u, 1], sum_sem, (u, 1), (by_a, v)
        )

    def sum_second(u):
        if u in DIRECT_SUM:
            return
        a, b, by_a, by_b = axes(u)
        sums[u, 0].wait_recv()
        passed[u] = (
            part[u, quarter(a, 1 - b), :].astype(F32) + first_in[u, 0].astype(F32)
        ).astype(BF16)
        sums[u, 2] = copy(passed.at[u], second_in.at[u], sum_sem, (u, 2), (by_b, v))

    def sum_third(u):
        a, b, by_a, by_b = axes(u)
        total = part[u, quarter(a, b), :].astype(F32)
        sums[u, 1].wait_recv()
        total += first_in[u, 1].astype(F32)
        if u in DIRECT_SUM:
            sums[u, 0].wait_recv()
            total += first_in[u, 0].astype(F32)
        sums[u, 2].wait_recv()
        zsum[u] = (total + second_in[u].astype(F32)).astype(BF16)
        for e in range(1, DEPTH):
            to = (z + e) % DEPTH
            sums[u, 2 + e] = copy(
                zsum.at[u, rows_at(to * piece, piece)], z_in.at[u, e - 1],
                z_sem, (u, e - 1), (to * PLANE + me % PLANE, v),
            )

    scale = math.sqrt(count * groups * full_width)
    spreads = {}

    def finish(u):
        a, b, by_a, by_b = axes(u)
        total = zsum[u, rows_at(z * piece, piece), :].astype(F32)
        for e in range(1, DEPTH):
            sums[u, 2 + e].wait_recv()
            total += z_in[u, e - 1].astype(F32)
        at = rows_at(((u * 2 + a) * 2 + b) * block + z * piece, piece)
        full[at, :] = (total / scale).astype(BF16)
        for e in range(1, DEPTH):
            spreads[u, e] = copy(
                full.at[at], full.at[at], gz_sem, (u, e - 1),
                ((z + e) % DEPTH * PLANE + me % PLANE, v),
            )

    def spread(u):
        a, b, by_a, by_b = axes(u)
        for e in range(1, DEPTH):
            spreads[u, e].wait_recv()
        at = rows_at(((u * 2 + a) * 2 + b) * block, block)
        ways = [by_b, by_a] + [by_xy] * (u in DIRECT_SPREAD)
        for i, to in enumerate(ways):
            spreads[u, DEPTH + i] = copy(full.at[at], full.at[at], spread_sem, (u, i), (to, v))

    def forward(u):
        if u in DIRECT_SPREAD:
            return
        a, b, by_a, by_b = axes(u)
        spreads[u, DEPTH].wait_recv()
        at = rows_at(((u * 2 + a) * 2 + 1 - b) * block, block)
        spreads[u, DEPTH + 2] = copy(full.at[at], full.at[at], spread_sem, (u, 2), (by_a, v))

    def done(u):
        if u in DIRECT_SPREAD:
            spreads[u, DEPTH].wait_recv()
        spreads[u, DEPTH + 1].wait_recv()
        spreads[u, DEPTH + 2].wait_recv()
        at = slice(u * unit, (u + 1) * unit)
        return (full[at, :].astype(F32) + gram[at, :]).astype(BF16)

    def energy():
        for t in range(count // 128):
            at = slice(t * 128, (t + 1) * 128)
            line = jnp.broadcast_to(occ_e[t : t + 1, :], (128, 128)).T
            for b in range(width // 128):
                cols = slice(b * 128, (b + 1) * 128)
                acc[at, cols] = (vir_e[:, cols] - line) * amp[at, cols].astype(F32)

    loads[2].wait()
    loads[3].wait()
    cross(0)
    cross(1)

    @pl.when(v == 0)
    def _():
        pl.semaphore_wait(barrier, 1 + 2 * near)
        pl.semaphore_signal(near_sem, inc=1, device_id=(me, 1), device_id_type=MESH)

    @pl.when(v == 1)
    def _():
        pl.semaphore_wait(near_sem, 1)

    sum_first(0)
    sum_first(1)
    amp_copies = []
    for i in range(2):
        at = pl.ds(i * unit, unit)
        amp_copies.append(copy(amp.at[:, at], other.at[:, at], amp_sem, (i,), (me, 1 - v)))
    loads[4].wait()
    loads[5].wait()
    energy()
    sum_second(0)
    sum_second(1)
    amp_copies[0].wait_recv()
    cross(2)
    sum_first(2)

    @pl.when(v == 1)
    def _():
        pl.semaphore_wait(barrier, 1 + 2 * (groups - 1 - near))
        pl.semaphore_signal(far_sem, inc=1, device_id=(me, 0), device_id_type=MESH)

    @pl.when(v == 0)
    def _():
        pl.semaphore_wait(far_sem, 1)

    amp_copies[1].wait_recv()
    cross(3)
    sum_first(3)
    sum_third(0)
    sum_third(1)
    route_copies = []
    for k in range(1, groups):
        to = (me + k) % groups
        route_copies.append(
            copy(outgoing.at[rows_at(to * capacity, capacity)], arr.at[mine], route_sem, (k - 1,), (to, v))
        )
    sum_second(2)
    sum_second(3)
    finish(0)
    finish(1)
    sum_third(2)
    sum_third(3)
    spread(0)
    spread(1)
    for c in route_copies:
        c.wait_recv()
    arr_copy = copy(arr, arr_o, arr_sem, (0,), (me, 1 - v))
    finish(2)
    finish(3)
    forward(0)
    forward(1)
    ladder = math.sqrt(full_width) * math.sqrt(SLOTS)
    contract = (((0,), (0,)), ((), ()))
    gram[:width, :] = lax.dot_general(arr[...], arr[...], contract, preferred_element_type=F32) / ladder
    arr_copy.wait_recv()
    gram[width:, :] = lax.dot_general(arr_o[...], arr[...], contract, preferred_element_type=F32) / ladder
    spread(2)
    spread(3)
    acc[...] += jnp.dot(amp[:, :unit], done(0), preferred_element_type=F32)
    acc[...] += jnp.dot(amp[:, unit:], done(1), preferred_element_type=F32)
    forward(2)
    forward(3)
    acc[...] += jnp.dot(other[:, :unit], done(2), preferred_element_type=F32)
    last[...] = done(3)
    for c in started:
        c.wait_send()


def finish_kernel(other, acc, last, out, held, sem):
    count, width = acc.shape
    unit = last.shape[0]
    tile = 512
    copies = []
    for t in range(count // tile):
        at = slice(t * tile, (t + 1) * tile)
        held[at, :] = (
            acc[at, :] + jnp.dot(other[at, width - unit :], last[...], preferred_element_type=F32)
        ).astype(BF16)
        c = pltpu.make_async_copy(held.at[pl.ds(t * tile, tile)], out.at[pl.ds(t * tile, tile)], sem.at[t])
        c.start()
        copies.append(c)
    for c in copies:
        c.wait()


def fused(amplitudes, cycle_ints, int_rows, row_dest, vir_energy, occ_energy):
    count, width = amplitudes.shape
    groups = DEPTH * PLANE
    unit = 2 * width // UNITS
    block = unit // PLANE
    dma = pltpu.SemaphoreType.DMA
    vmem = pl.BlockSpec(memory_space=pltpu.VMEM)
    other, acc, last = pl.pallas_call(
        kernel,
        out_shape=(
            pltpu.VMEM((count, width), BF16),
            pltpu.VMEM((count, width), F32),
            pltpu.VMEM((unit, width), BF16),
        ),
        in_specs=[pl.BlockSpec(memory_space=pltpu.HBM)] * 6,
        out_specs=[vmem] * 3,
        scratch_shapes=[
            pltpu.VMEM((count, width), BF16),
            pltpu.VMEM((count, width), BF16),
            pltpu.VMEM(int_rows.shape, BF16),
            pltpu.VMEM(row_dest.shape[::-1], jnp.int32),
            pltpu.VMEM((1, width), F32),
            pltpu.VMEM((count // 128, 128), F32),
            pltpu.VMEM((UNITS, unit, width), BF16),
            pltpu.VMEM((UNITS, 2, block, width), BF16),
            pltpu.VMEM((UNITS, block, width), BF16),
            pltpu.VMEM((UNITS, block, width), BF16),
            pltpu.VMEM((UNITS, block, width), BF16),
            pltpu.VMEM((UNITS, DEPTH - 1, block // DEPTH, width), BF16),
            pltpu.VMEM((2 * width, width), BF16),
            pltpu.VMEM((SLOTS, width), BF16),
            pltpu.VMEM((SLOTS, width), BF16),
            pltpu.VMEM((SLOTS, width), BF16),
            pltpu.VMEM((2 * width, width), F32),
            pltpu.SemaphoreType.REGULAR,
            pltpu.SemaphoreType.REGULAR,
            dma((6,)),
            dma((2, 2)),
            dma((2, groups - 1)),
            dma((2, 1)),
            dma((2, UNITS, 3)),
            dma((2, UNITS, DEPTH - 1)),
            dma((2, UNITS, DEPTH - 1)),
            dma((2, UNITS, 3)),
        ],
        compiler_params=pltpu.CompilerParams(
            collective_id=0, has_side_effects=True, vmem_limit_bytes=56 * 2**20
        ),
    )(
        amplitudes, cycle_ints, int_rows, row_dest.T,
        vir_energy.reshape(1, width), occ_energy.reshape(count // 128, 128),
    )
    return pl.pallas_call(
        finish_kernel,
        out_shape=jax.ShapeDtypeStruct((count, width), BF16),
        in_specs=[vmem] * 3,
        out_specs=pl.BlockSpec(memory_space=pltpu.HBM),
        scratch_shapes=[pltpu.VMEM((count, width), BF16), dma((count // 512,))],
        compiler_params=pltpu.CompilerParams(vmem_limit_bytes=24 * 2**20),
    )(other, acc, last)


def solution(mesh):
    fits = mesh.shape["pair"] == DEPTH * PLANE and mesh.shape["vir"] == 2
    return jax.shard_map(
        fused if fits else body,
        mesh=mesh,
        in_specs=(
            P("pair", "vir"),
            P("pair", "vir"),
            P("pair", "vir"),
            P("pair", None),
            P("vir"),
            P("pair"),
        ),
        out_specs=P("pair", "vir"),
        check_vma=False,
    )
```

time: 46.9 us -> 45.2 us (0.964)
  local copies, waits for them, and re-layouts: 3.4 us -> 0 us
  Pallas kernels: 43.4 us -> 45 us
    unnamed x1 -> x0, local copies, waits for them, and re-layouts: 3.4 us -> none
    pallas_call x1 -> x2, Pallas kernels: 43.4 us -> 45 us  [the longest x1 43.2 us: fused(): pl.pallas_call(kernel, out_shape=(pltpu.VMEM((count, width), BF16), pltpu...]
where the time goes in v1:
time: 45.2 us; the launch traced here: 45 us
  Pallas kernels  45 us (100%)
    pallas_call x1, Pallas kernels, fused(): pl.pallas_call(kernel, out_shape=(pltpu.VMEM((count, width), BF16), pltpu...  43.2 us
    pallas_call x1, Pallas kernels, fused(): pl.pallas_call(finish_kernel, out_shape=jax.ShapeDtypeStruct((count, widt...  1.83 us

profile of v1, /device:TPU:0, one launch (start us, length us, event | category | flops | bytes accessed | tf_op | source)
XLA Modules:
  0.0 45.0 jit_solution(16912574463330757746)
XLA Ops:
  0.0 43.2 %shard_map.64 = (bf16[2560,512]{1,0:T(8,128)(2,1)S(1)}, f32[2560,512]{1,0:T(8,128)S(1)}, bf16[256,512]{1,0:T(8,128)(2,1)S(1)}) custom-call(bf16[2560,512]{1,0:T(8,128)(2,1)} %amp_hbm.1, bf16[2560,512]{1,0:T(8,128)(2,1)} %cyc_hbm.1, bf16[64,512]{1,0:T(8,128)(2,1)} %rows_hbm.1, s32[2,64]{1,0:T(2,128)} %bitcast.5, f32[1,512]{1,0:T(1,128)} %bitcast.4, ...), custom_call_target="tpu_custom_call" | custom-call | tf_op jit(solution)/shard_map/pallas_call | solution.py:354
  43.2 1.8 %shard_map.65 = bf16[2560,512]{1,0:T(8,128)(2,1)} custom-call(bf16[2560,512]{1,0:T(8,128)(2,1)S(1)} %get-tuple-element.8.other, f32[2560,512]{1,0:T(8,128)S(1)} %get-tuple-element.9.acc, bf16[256,512]{1,0:T(8,128)(2,1)S(1)} %get-tuple-element.10.last), custom_call_target="tpu_custom_call" | custom-call | tf_op jit(solution)/shard_map/pallas_call | solution.py:399

commit v2 on v1

--- a/solution.py
+++ b/solution.py
@@ -56,8 +56,6 @@
 
 
 DEPTH, PLANE, UNITS = 4, 4, 4
-DIRECT_SUM = ()
-DIRECT_SPREAD = (3,)
 F32, BF16 = jnp.float32, jnp.bfloat16
 MESH = pl.DeviceIdType.MESH
 
@@ -68,9 +66,9 @@
 
 def kernel(
     amp_hbm, cyc_hbm, rows_hbm, dest_hbm, vir_hbm, occ_hbm, other, acc, last,
-    amp, cyc, rows, dest, vir_e, occ_e, part, first_in, passed, second_in, zsum, z_in, full,
-    outgoing, arr, arr_o, gram,
-    near_sem, far_sem, load_sem, amp_sem, route_sem, arr_sem, sum_sem, z_sem, gz_sem, spread_sem,
+    amp, cyc, rows, dest, vir_e, occ_e, part, first_in, second_in, zsum, z_in, full,
+    outgoing, mid, arr, arr_o, gram,
+    core_sem, near_sem, hop_sem, load_sem, amp_sem, route_sem, arr_sem, sum_sem, z_sem, gz_sem, spread_sem,
 ):
     groups = DEPTH * PLANE
     me, v = lax.axis_index("pair"), lax.axis_index("vir")
@@ -83,25 +81,50 @@
     block = unit // PLANE
     piece = block // DEPTH
 
+    left, right = pl.ds(0, unit), pl.ds(unit, unit)
     loads = [
         pltpu.make_async_copy(src, dst, load_sem.at[i])
         for i, (src, dst) in enumerate(
             (
-                (dest_hbm, dest), (rows_hbm, rows), (amp_hbm, amp), (cyc_hbm, cyc),
-                (vir_hbm, vir_e), (occ_hbm, occ_e),
+                (cyc_hbm, cyc), (amp_hbm.at[:, left], amp.at[:, left]), (amp_hbm.at[:, right], amp.at[:, right]),
+                (dest_hbm, dest), (rows_hbm, rows), (vir_hbm, vir_e), (occ_hbm, occ_e),
             )
         )
     ]
-    barrier = pltpu.get_barrier_semaphore()
-    pl.semaphore_signal(barrier, inc=1, device_id=(me, 1 - v), device_id_type=MESH)
-    for k in range(1, groups):
-        to = (me + k) % groups
-        hops = jnp.abs(to // PLANE - z) + jnp.abs(to % PLANE // 2 - y) + jnp.abs(to % 2 - x)
-        core = jnp.where(hops == 1, 0, 1)
-        pl.semaphore_signal(barrier, inc=1, device_id=(to, core), device_id_type=MESH)
-    near = 2 + jnp.where(z > 0, 1, 0) + jnp.where(z < DEPTH - 1, 1, 0)
     for c in loads:
         c.start()
+
+    def signal(sem, to, core):
+        pl.semaphore_signal(sem, inc=1, device_id=(to, core), device_id_type=MESH)
+
+    def signal_depth(sem, core):
+        @pl.when(z > 0)
+        def _():
+            signal(sem, me - PLANE, core)
+
+        @pl.when(z < DEPTH - 1)
+        def _():
+            signal(sem, me + PLANE, core)
+
+    barrier = pltpu.get_barrier_semaphore()
+
+    @pl.when(v == 1)
+    def _():
+        signal(barrier, me, 0)
+
+    signal(barrier, by_x, 1)
+    signal(barrier, by_y, 1)
+    signal_depth(barrier, 1)
+    ends = jnp.where(z > 0, 1, 0) + jnp.where(z < DEPTH - 1, 1, 0)
+
+    @pl.when(v == 0)
+    def _():
+        pl.semaphore_wait(barrier, 1)
+        signal(core_sem, me, 1)
+
+    @pl.when(v == 1)
+    def _():
+        pl.semaphore_wait(core_sem, 1)
 
     started = []
 
@@ -118,24 +141,38 @@
         started.append(c)
         return c
 
-    loads[0].wait()
-    loads[1].wait()
-    group = lax.broadcasted_iota(jnp.int32, (SLOTS, rows.shape[0]), 0) // capacity
-    slot = lax.broadcasted_iota(jnp.int32, (SLOTS, rows.shape[0]), 0) % capacity
-    member = group == dest[0:1, :]
-    for k in range(1, dest.shape[0]):
-        member = member | (group == dest[k : k + 1, :])
-    tri = (rows.shape[0], rows.shape[0])
-    before = lax.broadcasted_iota(jnp.int32, tri, 0) < lax.broadcasted_iota(jnp.int32, tri, 1)
-    rank = jnp.dot(
-        jnp.where(member, 1.0, 0.0).astype(BF16),
-        jnp.where(before, 1.0, 0.0).astype(BF16),
-        preferred_element_type=F32,
-    )
-    select = jnp.where(member & (rank == slot.astype(F32)), 1.0, 0.0).astype(BF16)
-    outgoing[...] = jnp.dot(select, rows[...], preferred_element_type=F32).astype(BF16)
-    mine = rows_at(me * capacity, capacity)
-    arr[mine, :] = outgoing[mine, :]
+    def dispatch():
+        group = lax.broadcasted_iota(jnp.int32, (SLOTS, rows.shape[0]), 0) // capacity
+        slot = lax.broadcasted_iota(jnp.int32, (SLOTS, rows.shape[0]), 0) % capacity
+        member = group == dest[0:1, :]
+        for k in range(1, dest.shape[0]):
+            member = member | (group == dest[k : k + 1, :])
+        tri = (rows.shape[0], rows.shape[0])
+        before = lax.broadcasted_iota(jnp.int32, tri, 0) < lax.broadcasted_iota(jnp.int32, tri, 1)
+        rank = jnp.dot(
+            jnp.where(member, 1.0, 0.0).astype(BF16),
+            jnp.where(before, 1.0, 0.0).astype(BF16),
+            preferred_element_type=F32,
+        )
+        select = jnp.where(member & (rank == slot.astype(F32)), 1.0, 0.0).astype(BF16)
+        outgoing[...] = jnp.dot(select, rows[...], preferred_element_type=F32).astype(BF16).reshape(outgoing.shape)
+
+    def route_depth():
+        mid[z] = outgoing[z]
+        return [
+            copy(outgoing.at[(z + e) % DEPTH], mid.at[z], route_sem, (0, e - 1), ((z + e) % DEPTH * PLANE + me % PLANE, v))
+            for e in range(1, DEPTH)
+        ]
+
+    def route_plane():
+        for c in routed:
+            c.wait_recv()
+        q = me % PLANE
+        arr[:, q] = mid[:, q]
+        return [
+            copy(mid.at[:, to % PLANE], arr.at[:, q], route_sem, (1, i), (to, v))
+            for i, to in enumerate((by_x, by_y, by_xy))
+        ]
 
     def cross(u):
         src = amp if u < UNITS // 2 else other
@@ -154,39 +191,26 @@
 
     def sum_first(u):
         a, b, by_a, by_b = axes(u)
-        if u in DIRECT_SUM:
-            sums[u, 0] = copy(
-                part.at[u, quarter(1 - a, 1 - b)], first_in.at[u, 0], sum_sem, (u, 0), (by_xy, v)
-            )
-            sums[u, 2] = copy(
-                part.at[u, quarter(a, 1 - b)], second_in.at[u], sum_sem, (u, 2), (by_b, v)
-            )
-        else:
-            sums[u, 0] = copy(
-                part.at[u, quarter(1 - a, 1 - b)], first_in.at[u, 0], sum_sem, (u, 0), (by_a, v)
-            )
+        sums[u, 2] = copy(
+            part.at[u, quarter(a, 1 - b)], second_in.at[u], sum_sem, (u, 2), (by_b, v)
+        )
         sums[u, 1] = copy(
             part.at[u, quarter(1 - a, b)], first_in.at[u, 1], sum_sem, (u, 1), (by_a, v)
         )
 
-    def sum_second(u):
-        if u in DIRECT_SUM:
-            return
+    def sum_across(u):
         a, b, by_a, by_b = axes(u)
-        sums[u, 0].wait_recv()
-        passed[u] = (
-            part[u, quarter(a, 1 - b), :].astype(F32) + first_in[u, 0].astype(F32)
-        ).astype(BF16)
-        sums[u, 2] = copy(passed.at[u], second_in.at[u], sum_sem, (u, 2), (by_b, v))
+        sums[u, 0] = copy(
+            part.at[u, quarter(1 - a, 1 - b)], first_in.at[u, 0], sum_sem, (u, 0), (by_xy, v)
+        )
 
     def sum_third(u):
         a, b, by_a, by_b = axes(u)
         total = part[u, quarter(a, b), :].astype(F32)
         sums[u, 1].wait_recv()
         total += first_in[u, 1].astype(F32)
-        if u in DIRECT_SUM:
-            sums[u, 0].wait_recv()
-            total += first_in[u, 0].astype(F32)
+        sums[u, 0].wait_recv()
+        total += first_in[u, 0].astype(F32)
         sums[u, 2].wait_recv()
         zsum[u] = (total + second_in[u].astype(F32)).astype(BF16)
         for e in range(1, DEPTH):
@@ -218,23 +242,13 @@
         for e in range(1, DEPTH):
             spreads[u, e].wait_recv()
         at = rows_at(((u * 2 + a) * 2 + b) * block, block)
-        ways = [by_b, by_a] + [by_xy] * (u in DIRECT_SPREAD)
+        ways = [by_b, by_a, by_xy]
         for i, to in enumerate(ways):
             spreads[u, DEPTH + i] = copy(full.at[at], full.at[at], spread_sem, (u, i), (to, v))
 
-    def forward(u):
-        if u in DIRECT_SPREAD:
-            return
-        a, b, by_a, by_b = axes(u)
-        spreads[u, DEPTH].wait_recv()
-        at = rows_at(((u * 2 + a) * 2 + 1 - b) * block, block)
-        spreads[u, DEPTH + 2] = copy(full.at[at], full.at[at], spread_sem, (u, 2), (by_a, v))
-
     def done(u):
-        if u in DIRECT_SPREAD:
-            spreads[u, DEPTH].wait_recv()
-        spreads[u, DEPTH + 1].wait_recv()
-        spreads[u, DEPTH + 2].wait_recv()
+        for i in range(3):
+            spreads[u, DEPTH + i].wait_recv()
         at = slice(u * unit, (u + 1) * unit)
         return (full[at, :].astype(F32) + gram[at, :]).astype(BF16)
 
@@ -246,81 +260,72 @@
                 cols = slice(b * 128, (b + 1) * 128)
                 acc[at, cols] = (vir_e[:, cols] - line) * amp[at, cols].astype(F32)
 
-    loads[2].wait()
-    loads[3].wait()
+    amp_copies = []
+    for i, at in enumerate((left, right)):
+        amp_copies.append(copy(amp_hbm.at[:, at], other.at[:, at], amp_sem, (i,), (me, 1 - v)))
+    loads[0].wait()
+    loads[1].wait()
     cross(0)
-    cross(1)
+
+    @pl.when(v == 1)
+    def _():
+        pl.semaphore_wait(barrier, 2 * (2 + ends))
+        signal(near_sem, me, 0)
 
     @pl.when(v == 0)
     def _():
-        pl.semaphore_wait(barrier, 1 + 2 * near)
-        pl.semaphore_signal(near_sem, inc=1, device_id=(me, 1), device_id_type=MESH)
-
-    @pl.when(v == 1)
-    def _():
         pl.semaphore_wait(near_sem, 1)
 
+    signal(hop_sem.at[0], by_x, v)
+    signal(hop_sem.at[0], by_y, v)
+    signal_depth(hop_sem.at[0], v)
     sum_first(0)
+    loads[2].wait()
+    cross(1)
     sum_first(1)
-    amp_copies = []
-    for i in range(2):
-        at = pl.ds(i * unit, unit)
-        amp_copies.append(copy(amp.at[:, at], other.at[:, at], amp_sem, (i,), (me, 1 - v)))
-    loads[4].wait()
-    loads[5].wait()
-    energy()
-    sum_second(0)
-    sum_second(1)
     amp_copies[0].wait_recv()
     cross(2)
     sum_first(2)
-
-    @pl.when(v == 1)
-    def _():
-        pl.semaphore_wait(barrier, 1 + 2 * (groups - 1 - near))
-        pl.semaphore_signal(far_sem, inc=1, device_id=(me, 0), device_id_type=MESH)
-
-    @pl.when(v == 0)
-    def _():
-        pl.semaphore_wait(far_sem, 1)
-
+    pl.semaphore_wait(hop_sem.at[0], 2 + ends)
+    signal_depth(hop_sem.at[1], v)
+    sum_across(0)
+    sum_across(1)
+    sum_across(2)
+    for c in loads[3:]:
+        c.wait()
+    dispatch()
     amp_copies[1].wait_recv()
     cross(3)
     sum_first(3)
+    sum_across(3)
+    pl.semaphore_wait(hop_sem.at[1], ends)
+    routed = route_depth()
+    energy()
     sum_third(0)
     sum_third(1)
-    route_copies = []
-    for k in range(1, groups):
-        to = (me + k) % groups
-        route_copies.append(
-            copy(outgoing.at[rows_at(to * capacity, capacity)], arr.at[mine], route_sem, (k - 1,), (to, v))
-        )
-    sum_second(2)
-    sum_second(3)
     finish(0)
     finish(1)
     sum_third(2)
     sum_third(3)
+    routed = route_plane()
     spread(0)
     spread(1)
-    for c in route_copies:
+    finish(2)
+    finish(3)
+    for c in routed:
         c.wait_recv()
     arr_copy = copy(arr, arr_o, arr_sem, (0,), (me, 1 - v))
-    finish(2)
-    finish(3)
-    forward(0)
-    forward(1)
     ladder = math.sqrt(full_width) * math.sqrt(SLOTS)
     contract = (((0,), (0,)), ((), ()))
-    gram[:width, :] = lax.dot_general(arr[...], arr[...], contract, preferred_element_type=F32) / ladder
-    arr_copy.wait_recv()
-    gram[width:, :] = lax.dot_general(arr_o[...], arr[...], contract, preferred_element_type=F32) / ladder
+    chosen = arr[...].reshape(SLOTS, width)
+    gram[:width, :] = lax.dot_general(chosen, chosen, contract, preferred_element_type=F32) / ladder
     spread(2)
     spread(3)
+    arr_copy.wait_recv()
+    chosen_o = arr_o[...].reshape(SLOTS, width)
+    gram[width:, :] = lax.dot_general(chosen_o, chosen, contract, preferred_element_type=F32) / ladder
     acc[...] += jnp.dot(amp[:, :unit], done(0), preferred_element_type=F32)
     acc[...] += jnp.dot(amp[:, unit:], done(1), preferred_element_type=F32)
-    forward(2)
-    forward(3)
     acc[...] += jnp.dot(other[:, :unit], done(2), preferred_element_type=F32)
     last[...] = done(3)
     for c in started:
@@ -371,18 +376,19 @@
             pltpu.VMEM((UNITS, 2, block, width), BF16),
             pltpu.VMEM((UNITS, block, width), BF16),
             pltpu.VMEM((UNITS, block, width), BF16),
-            pltpu.VMEM((UNITS, block, width), BF16),
             pltpu.VMEM((UNITS, DEPTH - 1, block // DEPTH, width), BF16),
             pltpu.VMEM((2 * width, width), BF16),
-            pltpu.VMEM((SLOTS, width), BF16),
-            pltpu.VMEM((SLOTS, width), BF16),
-            pltpu.VMEM((SLOTS, width), BF16),
+            pltpu.VMEM((DEPTH, PLANE, SLOTS // groups, width), BF16),
+            pltpu.VMEM((DEPTH, PLANE, SLOTS // groups, width), BF16),
+            pltpu.VMEM((DEPTH, PLANE, SLOTS // groups, width), BF16),
+            pltpu.VMEM((DEPTH, PLANE, SLOTS // groups, width), BF16),
             pltpu.VMEM((2 * width, width), F32),
             pltpu.SemaphoreType.REGULAR,
             pltpu.SemaphoreType.REGULAR,
-            dma((6,)),
+            pltpu.SemaphoreType.REGULAR((2,)),
+            dma((7,)),
             dma((2, 2)),
-            dma((2, groups - 1)),
+            dma((2, 2, 3)),
             dma((2, 1)),
             dma((2, UNITS, 3)),
             dma((2, UNITS, DEPTH - 1)),

time: 45.2 us -> 39.3 us (0.87)
  Pallas kernels: 45 us -> 39.2 us
    pallas_call x1, Pallas kernels: 43.2 us -> 37.3 us  [fused(): pl.pallas_call(kernel, out_shape=(pltpu.VMEM((count, width), BF16), pltpu...]
where the time goes in v2:
time: 39.3 us; the launch traced here: 39.2 us
  Pallas kernels  39.2 us (100%)
    pallas_call x1, Pallas kernels, fused(): pl.pallas_call(kernel, out_shape=(pltpu.VMEM((count, width), BF16), pltpu...  37.3 us
    pallas_call x1, Pallas kernels, fused(): pl.pallas_call(finish_kernel, out_shape=jax.ShapeDtypeStruct((count, widt...  1.83 us

profile of v2, /device:TPU:0, one launch (start us, length us, event | category | flops | bytes accessed | tf_op | source)
XLA Modules:
  0.0 39.2 jit_solution(17903273926227365099)
XLA Ops:
  0.0 37.3 %shard_map.64 = (bf16[2560,512]{1,0:T(8,128)(2,1)S(1)}, f32[2560,512]{1,0:T(8,128)S(1)}, bf16[256,512]{1,0:T(8,128)(2,1)S(1)}) custom-call(bf16[2560,512]{1,0:T(8,128)(2,1)} %amp_hbm.1, bf16[2560,512]{1,0:T(8,128)(2,1)} %cyc_hbm.1, bf16[64,512]{1,0:T(8,128)(2,1)} %rows_hbm.1, s32[2,64]{1,0:T(2,128)} %bitcast.5, f32[1,512]{1,0:T(1,128)} %bitcast.4, ...), custom_call_target="tpu_custom_call" | custom-call | tf_op jit(solution)/shard_map/pallas_call | solution.py:359
  37.3 1.8 %shard_map.65 = bf16[2560,512]{1,0:T(8,128)(2,1)} custom-call(bf16[2560,512]{1,0:T(8,128)(2,1)S(1)} %get-tuple-element.8.other, f32[2560,512]{1,0:T(8,128)S(1)} %get-tuple-element.9.acc, bf16[256,512]{1,0:T(8,128)(2,1)S(1)} %get-tuple-element.10.last), custom_call_target="tpu_custom_call" | custom-call | tf_op jit(solution)/shard_map/pallas_call | solution.py:405

commit v3 on v2

--- a/solution.py
+++ b/solution.py
@@ -157,17 +157,19 @@
         select = jnp.where(member & (rank == slot.astype(F32)), 1.0, 0.0).astype(BF16)
         outgoing[...] = jnp.dot(select, rows[...], preferred_element_type=F32).astype(BF16).reshape(outgoing.shape)
 
-    def route_depth():
-        mid[z] = outgoing[z]
-        return [
-            copy(outgoing.at[(z + e) % DEPTH], mid.at[z], route_sem, (0, e - 1), ((z + e) % DEPTH * PLANE + me % PLANE, v))
-            for e in range(1, DEPTH)
-        ]
+    routed = []
+
+    def route_depth(i):
+        to = (z + 1 - 2 * (z % 2), (z + 2) % DEPTH, DEPTH - 1 - z)[i]
+        routed.append(
+            copy(outgoing.at[to], mid.at[z], route_sem, (0, i), (to * PLANE + me % PLANE, v))
+        )
 
     def route_plane():
         for c in routed:
             c.wait_recv()
         q = me % PLANE
+        mid[z] = outgoing[z]
         arr[:, q] = mid[:, q]
         return [
             copy(mid.at[:, to % PLANE], arr.at[:, q], route_sem, (1, i), (to, v))
@@ -283,35 +285,35 @@
     loads[2].wait()
     cross(1)
     sum_first(1)
+    for c in loads[3:]:
+        c.wait()
+    dispatch()
+    route_depth(0)
+    pl.semaphore_wait(hop_sem.at[0], 2 + ends)
+    signal_depth(hop_sem.at[1], v)
+    route_depth(1)
+    sum_across(0)
     amp_copies[0].wait_recv()
     cross(2)
     sum_first(2)
-    pl.semaphore_wait(hop_sem.at[0], 2 + ends)
-    signal_depth(hop_sem.at[1], v)
-    sum_across(0)
     sum_across(1)
     sum_across(2)
-    for c in loads[3:]:
-        c.wait()
-    dispatch()
+    pl.semaphore_wait(hop_sem.at[1], ends)
+    route_depth(2)
     amp_copies[1].wait_recv()
     cross(3)
     sum_first(3)
     sum_across(3)
-    pl.semaphore_wait(hop_sem.at[1], ends)
-    routed = route_depth()
+    sum_third(0)
     energy()
-    sum_third(0)
+    routed = route_plane()
     sum_third(1)
+    sum_third(2)
     finish(0)
     finish(1)
-    sum_third(2)
     sum_third(3)
-    routed = route_plane()
     spread(0)
     spread(1)
-    finish(2)
-    finish(3)
     for c in routed:
         c.wait_recv()
     arr_copy = copy(arr, arr_o, arr_sem, (0,), (me, 1 - v))
@@ -319,6 +321,8 @@
     contract = (((0,), (0,)), ((), ()))
     chosen = arr[...].reshape(SLOTS, width)
     gram[:width, :] = lax.dot_general(chosen, chosen, contract, preferred_element_type=F32) / ladder
+    finish(2)
+    finish(3)
     spread(2)
     spread(3)
     arr_copy.wait_recv()

time: 39.3 us -> 37.8 us (0.962)
  Pallas kernels: 39.2 us -> 37.6 us
    pallas_call x1, Pallas kernels: 37.3 us -> 35.8 us  [fused(): pl.pallas_call(kernel, out_shape=(pltpu.VMEM((count, width), BF16), pltpu...]
where the time goes in v3:
time: 37.8 us; the launch traced here: 37.6 us
  Pallas kernels  37.6 us (99%)
    pallas_call x1, Pallas kernels, fused(): pl.pallas_call(kernel, out_shape=(pltpu.VMEM((count, width), BF16), pltpu...  35.8 us
    pallas_call x1, Pallas kernels, fused(): pl.pallas_call(finish_kernel, out_shape=jax.ShapeDtypeStruct((count, widt...  1.83 us

profile of v3, /device:TPU:0, one launch (start us, length us, event | category | flops | bytes accessed | tf_op | source)
XLA Modules:
  0.0 37.6 jit_solution(18183699932953821496)
XLA Ops:
  0.0 35.8 %shard_map.64 = (bf16[2560,512]{1,0:T(8,128)(2,1)S(1)}, f32[2560,512]{1,0:T(8,128)S(1)}, bf16[256,512]{1,0:T(8,128)(2,1)S(1)}) custom-call(bf16[2560,512]{1,0:T(8,128)(2,1)} %amp_hbm.1, bf16[2560,512]{1,0:T(8,128)(2,1)} %cyc_hbm.1, bf16[64,512]{1,0:T(8,128)(2,1)} %rows_hbm.1, s32[2,64]{1,0:T(2,128)} %bitcast.5, f32[1,512]{1,0:T(1,128)} %bitcast.4, ...), custom_call_target="tpu_custom_call" | custom-call | tf_op jit(solution)/shard_map/pallas_call | solution.py:363
  35.8 1.8 %shard_map.65 = bf16[2560,512]{1,0:T(8,128)(2,1)} custom-call(bf16[2560,512]{1,0:T(8,128)(2,1)S(1)} %get-tuple-element.8.other, f32[2560,512]{1,0:T(8,128)S(1)} %get-tuple-element.9.acc, bf16[256,512]{1,0:T(8,128)(2,1)S(1)} %get-tuple-element.10.last), custom_call_target="tpu_custom_call" | custom-call | tf_op jit(solution)/shard_map/pallas_call | solution.py:409

commit v4 on v3

--- a/solution.py
+++ b/solution.py
@@ -223,7 +223,7 @@
             )
 
     scale = math.sqrt(count * groups * full_width)
-    spreads = {}
+    spreads, planes = {}, {}
 
     def finish(u):
         a, b, by_a, by_b = axes(u)
@@ -239,18 +239,18 @@
                 ((z + e) % DEPTH * PLANE + me % PLANE, v),
             )
 
-    def spread(u):
+    def spread(u, e):
         a, b, by_a, by_b = axes(u)
-        for e in range(1, DEPTH):
+        if e:
             spreads[u, e].wait_recv()
-        at = rows_at(((u * 2 + a) * 2 + b) * block, block)
-        ways = [by_b, by_a, by_xy]
-        for i, to in enumerate(ways):
-            spreads[u, DEPTH + i] = copy(full.at[at], full.at[at], spread_sem, (u, i), (to, v))
+        at = rows_at(((u * 2 + a) * 2 + b) * block + (z - e + DEPTH) % DEPTH * piece, piece)
+        for i, to in enumerate((by_b, by_a, by_xy)):
+            planes[u, e, i] = copy(full.at[at], full.at[at], spread_sem, (u, e, i), (to, v))
 
     def done(u):
-        for i in range(3):
-            spreads[u, DEPTH + i].wait_recv()
+        for e in range(DEPTH):
+            for i in range(PLANE - 1):
+                planes[u, e, i].wait_recv()
         at = slice(u * unit, (u + 1) * unit)
         return (full[at, :].astype(F32) + gram[at, :]).astype(BF16)
 
@@ -285,18 +285,18 @@
     loads[2].wait()
     cross(1)
     sum_first(1)
+    pl.semaphore_wait(hop_sem.at[0], 2 + ends)
+    signal_depth(hop_sem.at[1], v)
+    sum_across(0)
+    sum_across(1)
     for c in loads[3:]:
         c.wait()
     dispatch()
     route_depth(0)
-    pl.semaphore_wait(hop_sem.at[0], 2 + ends)
-    signal_depth(hop_sem.at[1], v)
     route_depth(1)
-    sum_across(0)
     amp_copies[0].wait_recv()
     cross(2)
     sum_first(2)
-    sum_across(1)
     sum_across(2)
     pl.semaphore_wait(hop_sem.at[1], ends)
     route_depth(2)
@@ -305,15 +305,23 @@
     sum_first(3)
     sum_across(3)
     sum_third(0)
-    energy()
     routed = route_plane()
     sum_third(1)
+    energy()
     sum_third(2)
     finish(0)
+    spread(0, 0)
     finish(1)
+    spread(1, 0)
     sum_third(3)
-    spread(0)
-    spread(1)
+    finish(2)
+    spread(2, 0)
+    for e in range(1, DEPTH):
+        spread(0, e)
+    for e in range(1, DEPTH):
+        spread(1, e)
+    finish(3)
+    spread(3, 0)
     for c in routed:
         c.wait_recv()
     arr_copy = copy(arr, arr_o, arr_sem, (0,), (me, 1 - v))
@@ -321,10 +329,10 @@
     contract = (((0,), (0,)), ((), ()))
     chosen = arr[...].reshape(SLOTS, width)
     gram[:width, :] = lax.dot_general(chosen, chosen, contract, preferred_element_type=F32) / ladder
-    finish(2)
-    finish(3)
-    spread(2)
-    spread(3)
+    for e in range(1, DEPTH):
+        spread(2, e)
+    for e in range(1, DEPTH):
+        spread(3, e)
     arr_copy.wait_recv()
     chosen_o = arr_o[...].reshape(SLOTS, width)
     gram[width:, :] = lax.dot_general(chosen_o, chosen, contract, preferred_element_type=F32) / ladder
@@ -397,7 +405,7 @@
             dma((2, UNITS, 3)),
             dma((2, UNITS, DEPTH - 1)),
             dma((2, UNITS, DEPTH - 1)),
-            dma((2, UNITS, 3)),
+            dma((2, UNITS, DEPTH, PLANE - 1)),
         ],
         compiler_params=pltpu.CompilerParams(
             collective_id=0, has_side_effects=True, vmem_limit_bytes=56 * 2**20

time: 37.8 us -> 37 us (0.979)
  Pallas kernels: 37.6 us -> 36.9 us
    pallas_call x1, Pallas kernels: 35.8 us -> 35.1 us  [fused(): pl.pallas_call(kernel, out_shape=(pltpu.VMEM((count, width), BF16), pltpu...]
where the time goes in v4:
time: 37 us; the launch traced here: 36.9 us
  Pallas kernels  36.9 us (100%)
    pallas_call x1, Pallas kernels, fused(): pl.pallas_call(kernel, out_shape=(pltpu.VMEM((count, width), BF16), pltpu...  35.1 us
    pallas_call x1, Pallas kernels, fused(): pl.pallas_call(finish_kernel, out_shape=jax.ShapeDtypeStruct((count, widt...  1.83 us

profile of v4, /device:TPU:0, one launch (start us, length us, event | category | flops | bytes accessed | tf_op | source)
XLA Modules:
  0.0 36.9 jit_solution(6227283163380544090)
XLA Ops:
  0.0 35.1 %shard_map.64 = (bf16[2560,512]{1,0:T(8,128)(2,1)S(1)}, f32[2560,512]{1,0:T(8,128)S(1)}, bf16[256,512]{1,0:T(8,128)(2,1)S(1)}) custom-call(bf16[2560,512]{1,0:T(8,128)(2,1)} %amp_hbm.1, bf16[2560,512]{1,0:T(8,128)(2,1)} %cyc_hbm.1, bf16[64,512]{1,0:T(8,128)(2,1)} %rows_hbm.1, s32[2,64]{1,0:T(2,128)} %bitcast.5, f32[1,512]{1,0:T(1,128)} %bitcast.4, ...), custom_call_target="tpu_custom_call" | custom-call | tf_op jit(solution)/shard_map/pallas_call | solution.py:371
  35.1 1.8 %shard_map.65 = bf16[2560,512]{1,0:T(8,128)(2,1)} custom-call(bf16[2560,512]{1,0:T(8,128)(2,1)S(1)} %get-tuple-element.8.other, f32[2560,512]{1,0:T(8,128)S(1)} %get-tuple-element.9.acc, bf16[256,512]{1,0:T(8,128)(2,1)S(1)} %get-tuple-element.10.last), custom_call_target="tpu_custom_call" | custom-call | tf_op jit(solution)/shard_map/pallas_call | solution.py:417

commit v5 on v4

--- a/solution.py
+++ b/solution.py
@@ -244,7 +244,7 @@
         if e:
             spreads[u, e].wait_recv()
         at = rows_at(((u * 2 + a) * 2 + b) * block + (z - e + DEPTH) % DEPTH * piece, piece)
-        for i, to in enumerate((by_b, by_a, by_xy)):
+        for i, to in enumerate((by_xy, by_b, by_a)):
             planes[u, e, i] = copy(full.at[at], full.at[at], spread_sem, (u, e, i), (to, v))
 
     def done(u):
@@ -347,7 +347,7 @@
 def finish_kernel(other, acc, last, out, held, sem):
     count, width = acc.shape
     unit = last.shape[0]
-    tile = 512
+    tile = 256
     copies = []
     for t in range(count // tile):
         at = slice(t * tile, (t + 1) * tile)
@@ -419,7 +419,7 @@
         out_shape=jax.ShapeDtypeStruct((count, width), BF16),
         in_specs=[vmem] * 3,
         out_specs=pl.BlockSpec(memory_space=pltpu.HBM),
-        scratch_shapes=[pltpu.VMEM((count, width), BF16), dma((count // 512,))],
+        scratch_shapes=[pltpu.VMEM((count, width), BF16), dma((count // 256,))],
         compiler_params=pltpu.CompilerParams(vmem_limit_bytes=24 * 2**20),
     )(other, acc, last)
 

time: 37 us -> 36.8 us (level)
  no operation moved by 1% of the time
where the time goes in v5:
time: 36.8 us; the launch traced here: 36.7 us
  Pallas kernels  36.7 us (100%)
    pallas_call x1, Pallas kernels, fused(): pl.pallas_call(kernel, out_shape=(pltpu.VMEM((count, width), BF16), pltpu...  34.9 us
    pallas_call x1, Pallas kernels, fused(): pl.pallas_call(finish_kernel, out_shape=jax.ShapeDtypeStruct((count, widt...  1.8 us

profile of v5, /device:TPU:0, one launch (start us, length us, event | category | flops | bytes accessed | tf_op | source)
XLA Modules:
  0.0 36.7 jit_solution(5337822310594780842)
XLA Ops:
  0.0 34.9 %shard_map.64 = (bf16[2560,512]{1,0:T(8,128)(2,1)S(1)}, f32[2560,512]{1,0:T(8,128)S(1)}, bf16[256,512]{1,0:T(8,128)(2,1)S(1)}) custom-call(bf16[2560,512]{1,0:T(8,128)(2,1)} %amp_hbm.1, bf16[2560,512]{1,0:T(8,128)(2,1)} %cyc_hbm.1, bf16[64,512]{1,0:T(8,128)(2,1)} %rows_hbm.1, s32[2,64]{1,0:T(2,128)} %bitcast.5, f32[1,512]{1,0:T(1,128)} %bitcast.4, ...), custom_call_target="tpu_custom_call" | custom-call | tf_op jit(solution)/shard_map/pallas_call | solution.py:371
  34.9 1.8 %shard_map.65 = bf16[2560,512]{1,0:T(8,128)(2,1)} custom-call(bf16[2560,512]{1,0:T(8,128)(2,1)S(1)} %get-tuple-element.8.other, f32[2560,512]{1,0:T(8,128)S(1)} %get-tuple-element.9.acc, bf16[256,512]{1,0:T(8,128)(2,1)S(1)} %get-tuple-element.10.last), custom_call_target="tpu_custom_call" | custom-call | tf_op jit(solution)/shard_map/pallas_call | solution.py:417
